TPU v7x, 256 devices: a whole 4x4x8 slice. The times are simulated.
256 devices in a mesh: gz: 64 (over y_hi, x, z), gy: 4 (over y_lo, core).
Axes of the slice: x: 4, y: 4 (y_hi: 2, y_lo: 2; y = y_hi * 2 + y_lo), z: 8, core: 2. Of those that a mesh axis runs over, the one named last changes fastest.
Arguments:
- concentration: float32 [1024, 128, 128], P('gz', 'gy'), may hold values from -0.9 to 0.9
- cotangent: float32 [1024, 128, 128], P('gz', 'gy'), may hold values from -12 to 12
- w_in: float32 [32, 4], replicated, may hold values from -3 to 3
- b_in: float32 [32], replicated, may hold values from -1 to 1
- w_out: float32 [32], replicated, may hold values from -1 to 1
- b_out: float32 [], replicated, may hold values from -1 to 1
Outputs:
- grad_concentration: float32 [1024, 128, 128], P('gz', 'gy')
- grad_w_in: float32 [32, 4], replicated
- grad_b_in: float32 [32], replicated
- grad_w_out: float32 [32], replicated
- grad_b_out: float32 [], replicated
All inputs are finite; a program needn't handle non-finite values.
Results may differ from a plain program's by a relative error of at most 0.00055.
Values sent between devices are 32-bit elements; how exact they have to be, the bound alone decides.
A program may use at most 64 MiB of HBM per device.

v0:
```python
import math

import jax
import jax.numpy as jnp
from jax import lax
from jax.experimental import pallas as pl
from jax.experimental.pallas import tpu as pltpu
from jax.sharding import PartitionSpec as P

KAPPA = 0.5
STEP = 0.008
FLOOR = 0.05
HIGH = lax.Precision.HIGHEST
MESH = pl.DeviceIdType.MESH
F32 = jnp.float32
BF16 = jnp.bfloat16

WC = 7
WA = 4
R = 8
UNITS = 32
ROWS = UNITS * 8


DIRECTIONS = [(dz, dy) for dz in (0, -1, 1) for dy in (-1, 1, 0) if (dz, dy) != (0, 0)]


def iota(shape, dim):
    return lax.broadcasted_iota(jnp.int32, shape, dim)


def xp(v):
    return pltpu.roll(v, v.shape[1] - 1, 1)


def xm(v):
    return pltpu.roll(v, 1, 1)


def yp(v):
    return pltpu.roll(v, v.shape[0] - 1, 0)


def ym(v):
    return pltpu.roll(v, 1, 0)


def split(v):
    high = v.astype(BF16)
    return high, (v - high.astype(F32)).astype(BF16)


def dot(a, b, precision=None):
    return jnp.dot(a, b, preferred_element_type=F32, precision=precision)


def make_kernel(zl, yl, ng, ny, factor):
    nv = yl // 8
    yr = yl + 2 * R
    g1 = 4 if ng % 4 == 0 else 1
    size1 = g1 * ny
    size2 = ng // g1

    def kernel(
        conc, cot, w_in, b_in, w_out, b_out,
        out, out_wi, out_bi, out_wo, out_bo,
        C, A0, MU1, M1, SG1, C2, MU2, M2, SG2, RR, UU, VV, A1, H1, H2,
        WL, WOF, CT, UB, PACC, TACC, GACC, OUTV, RED, RED2, MSG, MSG2,
        send_sem, recv_sem, local_sem, rs_send, rs_recv, rs2_send, rs2_recv,
    ):
        gz = lax.axis_index("gz")
        gy = lax.axis_index("gy")

        def neighbour(dz, dy):
            return (lax.rem(gz + dz + ng, ng), lax.rem(gy + dy + ny, ny))

        block1 = gz // g1
        place1 = lax.rem(gz, g1) * ny + gy
        place2 = block1

        def peer1(k):
            q = lax.rem(place1 + k, size1)
            return q, (block1 * g1 + q // ny, lax.rem(q, ny))

        def peer2(k):
            q = lax.rem(place2 + k, size2)
            return q, (q * g1 + lax.rem(gz, g1), gy)

        local_c = pltpu.make_async_copy(
            conc, C.at[pl.ds(WC, zl), pl.ds(R, yl)], local_sem.at[0])
        local_a = pltpu.make_async_copy(
            cot, A0.at[pl.ds(WA, zl), pl.ds(R, yl)], local_sem.at[1])
        local_c.start()
        local_a.start()

        barrier = pltpu.get_barrier_semaphore()
        count = 0
        for dz, dy in DIRECTIONS:
            pl.semaphore_signal(barrier, inc=1, device_id=neighbour(dz, dy), device_id_type=MESH)
            count += 1
        for k in range(1, size1):
            pl.semaphore_signal(barrier, inc=1, device_id=peer1(k)[1], device_id_type=MESH)
            count += 1
        for k in range(1, size2):
            pl.semaphore_signal(barrier, inc=1, device_id=peer2(k)[1], device_id_type=MESH)
            count += 1
        pl.semaphore_wait(barrier, count)

        def span_z(dz, width):
            if dz > 0:
                return pl.ds(zl - width, width), pl.ds(0, width)
            if dz < 0:
                return pl.ds(0, width), pl.ds(width + zl, width)
            return pl.ds(0, zl), pl.ds(width, zl)

        def span_y(dy):
            if dy > 0:
                return pl.ds(yl - R, R), pl.ds(0, R)
            if dy < 0:
                return pl.ds(0, R), pl.ds(R + yl, R)
            return pl.ds(0, yl), pl.ds(R, yl)

        def halo(which, source, field, width):
            copies = []
            for n, (dz, dy) in enumerate(DIRECTIONS):
                sz, tz = span_z(dz, width)
                sy, ty = span_y(dy)
                copies.append(pltpu.make_async_remote_copy(
                    src_ref=source.at[sz, sy],
                    dst_ref=field.at[tz, ty],
                    send_sem=send_sem.at[which, n],
                    recv_sem=recv_sem.at[which, n],
                    device_id=neighbour(dz, dy),
                    device_id_type=MESH,
                ))
            return copies

        halo_c = halo(0, conc, C, WC)
        halo_a = halo(1, cot, A0, WA)
        for copy in halo_c:
            copy.start()
        for copy in halo_a:
            copy.start()

        lane = iota((UNITS, 128), 1)
        eye = iota((UNITS, UNITS), 0) == iota((UNITS, UNITS), 1)
        bi_col = jnp.sum(jnp.where(eye, b_in[...], 0.0), axis=1, keepdims=True)
        wo_col = jnp.sum(jnp.where(eye, w_out[...], 0.0), axis=1, keepdims=True)
        packed = jnp.where(lane == 4, bi_col, jnp.where(lane == 5, wo_col, 0.0))
        for k in range(4):
            packed = jnp.where(lane == k, w_in[:, k:k + 1], packed)
        spread = (iota((ROWS, UNITS), 0) // 8 == iota((ROWS, UNITS), 1)).astype(F32)
        params = dot(spread, packed, HIGH)
        row = iota((ROWS, 128), 0)
        col = iota((ROWS, 128), 1)
        same = (row & 7) == (col & 7)
        which_k = (col & 31) // 8
        group = col // 32
        w_sel = jnp.zeros((ROWS, 128), F32)
        for k in range(4):
            w_sel = jnp.where(which_k == k, params[:, k:k + 1], w_sel)
        bias = jnp.broadcast_to(params[:, 4:5], (ROWS, 128))
        wo_full = jnp.broadcast_to(params[:, 5:6], (ROWS, 128))
        WOF[...] = wo_full
        value = jnp.where(group == 3, jnp.where(which_k < 2, bias, 0.0), w_sel)
        high = value.astype(BF16).astype(F32)
        low = value - high
        is_low = (group == 1) | ((group == 3) & (which_k == 1))
        WL[...] = jnp.where(same, jnp.where(is_low, low, high), 0.0).astype(BF16)
        joint = w_sel * wo_full
        j_high = joint.astype(BF16).astype(F32)
        j_low = joint - j_high
        j_mat = jnp.where(same, jnp.where(group == 0, j_high, jnp.where(group == 1, j_low, 0.0)), 0.0)
        CT[...] = j_mat.T[0:64].astype(BF16)
        PACC[...] = jnp.zeros((2 * ROWS, 128), F32)
        TACC[...] = jnp.zeros((ROWS, 128), F32)
        GACC[...] = jnp.zeros((8, 128), F32)

        half = iota((8, 128), 0) < 4

        def pack(v):
            blocks = [v[R + 8 * i:R + 8 * i + 8] for i in range(nv)]
            blocks.append(jnp.where(half, v[R + yl:], v[:R]))
            return blocks

        def unpack(blocks):
            return jnp.concatenate([blocks[-1]] + blocks[:-1] + [blocks[-1]], axis=0)

        def fields_of(c_ref, p):
            c = c_ref[p]
            zu, zd = c_ref[p + 1], c_ref[p - 1]
            yu, yd = yp(c), ym(c)
            xu, xd = xp(c), xm(c)
            lap = ((zu + zd) + (yu + yd)) + (xu + xd) - 6.0 * c
            s0, s1, s2 = 0.5 * (zu - zd), 0.5 * (yu - yd), 0.5 * (xu - xd)
            sq = s0 * s0 + s1 * s1 + s2 * s2
            return c, lap, sq, (s0, s1, s2)

        def units(pair):
            feats = jnp.concatenate([jnp.concatenate(f, axis=0) for f in pair], axis=1)
            f_high, f_low = split(feats)
            rhs = jnp.concatenate([f_high, f_high, f_low, jnp.ones((32, 256), BF16)], axis=0)
            return jnp.tanh(dot(WL[...], rhs))

        def score(h):
            wo = WOF[...]
            weighted = h * jnp.concatenate([wo, wo], axis=1)
            return jnp.sum(weighted.reshape(UNITS, 8, 256), axis=0) + b_out[0, 0]

        def soft(s):
            e = jnp.exp(s)
            return jnp.log(1.0 + e) + FLOOR, e / (1.0 + e)

        def forward_one(p):
            for d in range(2):
                q = p + d
                c, lap, sq, _ = fields_of(C, q)
                mu = c * c * c - c - KAPPA * lap
                MU1[q] = mu
                feats = [c, lap, sq, mu]
                for a in range(0, nv + 2, 2):
                    ids = [1 + a, 2 + a] if a < nv else [nv + 1, 0]
                    pair = [[f[8 * i:8 * i + 8] for f in feats] for i in ids]
                    h = units(pair)
                    if a < nv:
                        H1[q, a] = h[:, :128]
                        H1[q, a + 1] = h[:, 128:]
                    else:
                        mask = (iota((ROWS, 128), 0) & 7) < 4
                        H1[q, nv] = jnp.where(mask, h[:, :128], h[:, 128:])
                    m, sg = soft(score(h))
                    for i in range(2):
                        rows = pl.ds(8 * ids[i], 8)
                        M1[q, rows] = m[:, 128 * i:128 * i + 128]
                        SG1[q, rows] = sg[:, 128 * i:128 * i + 128]

        def loop(first, last, body, step=2):
            def run(i, carry):
                body(first + step * i)
                return carry
            lax.fori_loop(0, (last - first) // step, run, 0)

        local_c.wait()
        for n in range(2):
            halo_c[n].wait_recv()
        loop(WC + 2, WC + zl - 2, forward_one)
        for n in range(2, 8):
            halo_c[n].wait_recv()
        loop(1, WC + 2, forward_one)
        loop(WC + zl - 2, 2 * WC + zl - 1, forward_one)

        def advance(p):
            mu, m = MU1[p], M1[p]
            def face(mu_a, m_a, mu_b, m_b):
                return (m_a + m_b) * (mu_b - mu_a)
            up = face(mu, m, MU1[p + 1], M1[p + 1])
            down = face(MU1[p - 1], M1[p - 1], mu, m)
            fy = face(mu, m, yp(mu), yp(m))
            fx = face(mu, m, xp(mu), xp(m))
            total = (up - down) + (fy - ym(fy)) + (fx - xm(fx))
            C2[p] = C[p] + (0.5 * STEP) * total

        loop(2, 2 * WC + zl - 2, advance, 1)

        def forward_two(p):
            feats = []
            for d in range(2):
                q = p + d
                c, lap, sq, _ = fields_of(C2, q)
                mu = c * c * c - c - KAPPA * lap
                MU2[q] = mu
                feats.append([pack(f) for f in (c, lap, sq, mu)])
            work = [((d, a), (d, a + 1)) for d in range(2) for a in range(0, nv, 2)] + [((0, nv), (1, nv))]
            for places in work:
                h = units([[f[a] for f in feats[d]] for d, a in places])
                m, sg = soft(score(h))
                for i, (d, a) in enumerate(places):
                    q = p + d
                    H2[q, a] = h[:, 128 * i:128 * i + 128]
                    mi, si = m[:, 128 * i:128 * i + 128], sg[:, 128 * i:128 * i + 128]
                    for start in ([R + 8 * a] if a < nv else [0, R + yl]):
                        M2[q, pl.ds(start, 8)] = mi
                        SG2[q, pl.ds(start, 8)] = si

        loop(3, 2 * WC + zl - 3, forward_two)

        def backward(p, adj, shift, c_ref, mu_ref, m_ref, sg_ref, h_ref):
            states = []
            for q in p:
                c, lap, sq, slopes = fields_of(c_ref, q)
                mu, m, a = mu_ref[q], m_ref[q], adj[q + shift]
                def faces(mu_a, m_a, a_a, mu_b, m_b, a_b):
                    da = a_b - a_a
                    return (mu_b - mu_a) * da, (m_a + m_b) * da
                q_up, r_up = faces(mu, m, a, mu_ref[q + 1], m_ref[q + 1], adj[q + 1 + shift])
                q_dn, r_dn = faces(mu_ref[q - 1], m_ref[q - 1], adj[q - 1 + shift], mu, m, a)
                q_y, r_y = faces(mu, m, a, yp(mu), yp(m), yp(a))
                q_x, r_x = faces(mu, m, a, xp(mu), xp(m), xp(a))
                adj_mob = (q_up + q_dn) + (q_y + ym(q_y)) + (q_x + xm(q_x))
                adj_pot = (r_up - r_dn) + (r_y - ym(r_y)) + (r_x - xm(r_x))
                g = (-0.5 * STEP) * adj_mob * sg_ref[q]
                adj_pot = (0.5 * STEP) * adj_pot
                states.append(dict(c=c, a=a, slopes=slopes, adj_pot=adj_pot, g=pack(g), f=[pack(f) for f in (c, lap, sq, mu)], A={}))

            work = [((d, b), (d, b + 1)) for d in range(2) for b in range(0, nv, 2)] + [((0, nv), (1, nv))]
            gg = []
            for n, places in enumerate(work):
                h = jnp.concatenate([h_ref[p[d], b] for d, b in places], axis=1)
                u = 1.0 - h * h
                u_high = u.astype(BF16)
                back = dot(CT[...], u_high)
                back = back[:32] + back[32:]
                g = jnp.concatenate([states[d]["g"][b] for d, b in places], axis=1)
                for i, (d, b) in enumerate(places):
                    states[d]["A"][b] = [
                        back[8 * k:8 * k + 8, 128 * i:128 * i + 128] * states[d]["g"][b] for k in range(4)
                    ]
                if n < len(work) - 1:
                    UB[pl.ds(0, ROWS), pl.ds(256 * n, 256)] = u_high
                    UB[pl.ds(ROWS, ROWS), pl.ds(256 * n, 256)] = (u - u_high.astype(F32)).astype(BF16)
                    feats = [jnp.concatenate([states[d]["f"][k][b] for d, b in places], axis=1) for k in range(4)]
                    stack = jnp.concatenate([g * f for f in feats] + [g, jnp.zeros((8, 256), F32)], axis=0)
                    s_high, s_low = split(stack)
                    gg.append(jnp.concatenate([s_high, s_low, jnp.zeros((32, 256), BF16)], axis=0))
            return states, gg

        def sums(p, states, gg, h_ref):
            rhs = jnp.concatenate(gg, axis=1)
            PACC[...] += lax.dot_general(
                UB[...], rhs, (((1,), (1,)), ((), ())), preferred_element_type=F32)
            total = TACC[...].reshape(UNITS, 8, 128)
            g_total = GACC[...]
            for d in range(2):
                for b in range(nv):
                    g = states[d]["g"][b]
                    total = total + h_ref[p[d], b].reshape(UNITS, 8, 128) * g[None]
                    g_total = g_total + g
            TACC[...] = total.reshape(ROWS, 128)
            GACC[...] = g_total

        def finish(p, states):
            for d in range(2):
                s = states[d]
                A = [unpack([s["A"][b][k] for b in range(nv + 1)]) for k in range(4)]
                adj_pot = s["adj_pot"] + A[3]
                adj_lap = A[1] - KAPPA * adj_pot
                zed, why, ex = (A[2] * slope for slope in s["slopes"])
                rest = s["a"] + A[0] + (3.0 * s["c"] * s["c"] - 1.0) * adj_pot - 6.0 * adj_lap
                rest = rest + (xm(adj_lap + ex) + xp(adj_lap - ex)) + (ym(adj_lap + why) + yp(adj_lap - why))
                RR[p[d]] = rest
                UU[p[d]] = adj_lap + zed
                VV[p[d]] = adj_lap - zed

        for copy in halo_a:
            copy.wait_recv()
        local_a.wait()

        def back_two(with_sums):
            def body(p):
                states, gg = backward(p, A0, WA - WC, C2, MU2, M2, SG2, H2)
                if with_sums:
                    sums(p, states, gg, H2)
                finish(p, states)
            return body

        def back_one(with_sums):
            def body(p):
                states, gg = backward(p, A1, 0, C, MU1, M1, SG1, H1)
                if with_sums:
                    sums(p, states, gg, H1)
                finish(p, states)
            return body

        loop(0, 3, lambda k: back_two(False)((WC - 1 - k, WC + zl + k)), 1)
        loop(WC, WC + zl, lambda p: back_two(True)((p, p + 1)))

        def join(p):
            A1[p] = RR[p] + UU[p - 1] + VV[p + 1]

        loop(WC - 2, WC + zl + 2, join, 1)

        loop(WC, WC + zl, lambda p: back_one(True)((p, p + 1)))
        back_one(False)((WC - 1, WC + zl))

        both = PACC[pl.ds(0, ROWS)] + PACC[pl.ds(ROWS, ROWS)]
        both = jnp.where(same & (col < 96), both, 0.0)
        gather = (iota((UNITS, ROWS), 1) // 8 == iota((UNITS, ROWS), 0)).astype(F32)
        by_unit = dot(gather, both, HIGH)
        c_row = iota((128, 128), 0)
        c_col = iota((128, 128), 1)
        c_k = jnp.where(c_row < 48, c_row, c_row - 48) // 8
        collect = ((c_k == c_col) & (c_row < 96) & (c_col < 5)).astype(F32)
        grads = dot(by_unit, collect, HIGH) * wo_col
        t_col = jnp.sum(dot(gather, TACC[...], HIGH), axis=1, keepdims=True)
        g_sum = jnp.sum(jnp.sum(GACC[...], axis=0, keepdims=True), axis=1, keepdims=True)
        first_row = iota((UNITS, 128), 0) == 0
        grads = jnp.where(lane == 5, t_col, grads)
        grads = jnp.where((lane == 6) & first_row, g_sum, grads)
        message = grads[0:8]
        for n in range(1, 4):
            message = message + pltpu.roll(grads[8 * n:8 * n + 8], 32 * n, 1)
        MSG[...] = message

        def exchange(size, place, peer, src, slots, s_sem, r_sem):
            copies = []
            for k in range(1, size):
                q, device = peer(k)
                copy = pltpu.make_async_remote_copy(
                    src_ref=src, dst_ref=slots.at[place], send_sem=s_sem.at[k],
                    recv_sem=r_sem.at[place], device_id=device, device_id_type=MESH)
                copy.start()
                copies.append(copy)
            slots[place] = src[...]
            return copies

        def collected(size, peer, copies, src, slots, s_sem, r_sem):
            for k in range(1, size):
                q, device = peer(k)
                pltpu.make_async_remote_copy(
                    src_ref=src, dst_ref=slots.at[q], send_sem=s_sem.at[k],
                    recv_sem=r_sem.at[q], device_id=device, device_id_type=MESH).wait_recv()
            total = slots[0]
            for k in range(1, size):
                total = total + slots[k]
            return total

        sent1 = exchange(size1, place1, peer1, MSG, RED, rs_send, rs_recv)

        def result(p):
            rows = pl.ds(R, yl)
            OUTV[p - WC] = RR[p, rows] + UU[p - 1, rows] + VV[p + 1, rows]

        loop(WC, WC + zl, result, 1)
        write = pltpu.make_async_copy(OUTV, out, local_sem.at[2])
        write.start()

        total = collected(size1, peer1, sent1, MSG, RED, rs_send, rs_recv)
        MSG2[...] = total
        if size2 > 1:
            sent2 = exchange(size2, place2, peer2, MSG2, RED2, rs2_send, rs2_recv)
            total = collected(size2, peer2, sent2, MSG2, RED2, rs2_send, rs2_recv)
        else:
            sent2 = []
        total = total * factor
        full = jnp.concatenate([total] + [pltpu.roll(total, 128 - 32 * n, 1) for n in range(1, 4)], axis=0)
        out_wi[...] = full[:, 0:4]
        out_bi[...] = jnp.sum(jnp.where(eye, full[:, 4:5], 0.0), axis=0, keepdims=True)
        out_wo[...] = jnp.sum(jnp.where(eye, full[:, 5:6], 0.0), axis=0, keepdims=True)
        out_bo[...] = full[0:1, 6:7]

        for copy in halo_c + halo_a + sent1 + sent2:
            copy.wait_send()
        write.wait()

    return kernel, yr, size1, size2


def per_device(ng, ny, concentration, cotangent, w_in, b_in, w_out, b_out):
    zl, yl, nx = concentration.shape
    factor = 1.0 / (STEP * math.sqrt(float(zl * yl * nx * ng * ny)))
    kernel, yr, size1, size2 = make_kernel(zl, yl, ng, ny, factor)
    planes = zl + 2 * WC
    nv = yl // 8
    field = pltpu.VMEM((planes, yr, nx), F32)
    anywhere = pl.BlockSpec(memory_space=pl.ANY)
    vmem = pl.BlockSpec(memory_space=pltpu.VMEM)
    smem = pl.BlockSpec(memory_space=pltpu.SMEM)
    outs = pl.pallas_call(
        kernel,
        out_shape=(
            jax.ShapeDtypeStruct(concentration.shape, F32),
            jax.ShapeDtypeStruct((UNITS, 4), F32),
            jax.ShapeDtypeStruct((1, UNITS), F32),
            jax.ShapeDtypeStruct((1, UNITS), F32),
            jax.ShapeDtypeStruct((1, 1), F32),
        ),
        in_specs=[anywhere, anywhere, vmem, vmem, vmem, smem],
        out_specs=(anywhere, vmem, vmem, vmem, vmem),
        scratch_shapes=[
            field,
            pltpu.VMEM((zl + 2 * WA, yr, nx), F32),
            field, field, field,
            field, field, field, field,
            field, field, field, field,
            pltpu.VMEM((planes, nv + 1, ROWS, nx), F32),
            pltpu.VMEM((planes, nv + 1, ROWS, nx), F32),
            pltpu.VMEM((ROWS, 128), BF16),
            pltpu.VMEM((ROWS, 128), F32),
            pltpu.VMEM((64, ROWS), BF16),
            pltpu.VMEM((2 * ROWS, 2 * yl // 8 * 128), BF16),
            pltpu.VMEM((2 * ROWS, 128), F32),
            pltpu.VMEM((ROWS, 128), F32),
            pltpu.VMEM((8, 128), F32),
            pltpu.VMEM((zl, yl, nx), F32),
            pltpu.VMEM((size1, 8, 128), F32),
            pltpu.VMEM((max(size2, 1), 8, 128), F32),
            pltpu.VMEM((8, 128), F32),
            pltpu.VMEM((8, 128), F32),
            pltpu.SemaphoreType.DMA((2, 8)),
            pltpu.SemaphoreType.DMA((2, 8)),
            pltpu.SemaphoreType.DMA((3,)),
            pltpu.SemaphoreType.DMA((size1,)),
            pltpu.SemaphoreType.DMA((size1,)),
            pltpu.SemaphoreType.DMA((size2,)),
            pltpu.SemaphoreType.DMA((size2,)),
        ],
        compiler_params=pltpu.CompilerParams(
            collective_id=0, has_side_effects=True, vmem_limit_bytes=60 * 1024 * 1024
        ),
    )(
        concentration, cotangent, w_in, b_in.reshape(1, UNITS), w_out.reshape(1, UNITS), b_out.reshape(1, 1)
    )
    return (outs[0], outs[1], outs[2].reshape(UNITS), outs[3].reshape(UNITS), outs[4].reshape(()))


def solution(mesh):
    ng, ny = mesh.shape["gz"], mesh.shape["gy"]
    in_specs = (P("gz", "gy", None), P("gz", "gy", None), P(), P(), P(), P())
    out_specs = (P("gz", "gy", None), P(), P(), P(), P())

    def run(*args):
        return per_device(ng, ny, *args)

    return jax.shard_map(run, mesh=mesh, in_specs=in_specs, out_specs=out_specs, check_vma=False)
```

profile of v0, /device:TPU:1, one launch (start us, length us, event | category | flops | bytes accessed | tf_op | source)
XLA Modules:
  0.0 73.2 jit_solution(9872908796710302276)
XLA Ops:
  1.3 0.0 copy-start
  1.3 0.7 copy-done
  2.0 0.7 copy.11.w_in
  2.7 64.6 %shard_map.101 = (f32[16,32,128]{2,1,0:T(8,128)}, f32[32,4]{1,0:T(8,128)}, f32[1,32]{1,0:T(1,128)}, f32[1,32]{1,0:T(1,128)}, f32[1,1]{1,0:T(1,128)}) custom-call(f32[16,32,128]{2,1,0:T(8,128)} %conc.1, f32[16,32,128]{2,1,0:T(8,128)} %cot.1, f32[32,4]{1,0:T(8,128)} %copy.11.w_in, f32[1,32]{1,0:T(1,128)} %bitcast.7, f32[1,32]{1,0:T(1,128)} %bitcast.8, ...), custom_call_target="tpu_custom_call" | custom-call | tf_op jit(solution)/shard_map/pallas_call | solution.py:468
  67.3 1.4 %copy.12 = f32[32,4]{0,1:T(4,128)} copy(f32[32,4]{1,0:T(8,128)} %get-tuple-element.16) | data formatting | bytes 1024
  68.6 0.0 copy-start.2
  68.6 1.7 %copy.18 = f32[16,32,128]{2,1,0:T(8,128)} copy(f32[16,32,128]{2,1,0:T(8,128)} %get-tuple-element.25) | data formatting | bytes 524288
  70.3 0.0 copy-done.2
  70.3 0.0 copy-start.1
  70.3 0.5 copy.19
  70.8 0.1 copy-done.1
  70.9 0.5 copy.20
Async XLA Ops:
  1.3 0.7 copy-start
  68.6 1.7 %copy-start.2 = (f32[1,32]{1,0:T(1,128)S(1)}, f32[1,32]{1,0:T(1,128)}, u32[]{:S(2)}) copy-start(f32[1,32]{1,0:T(1,128)} %get-tuple-element.12) | copy-start | bytes 388
  70.3 0.6 copy-start.1
where the time goes:
time: 73.4 us; the launch traced here: 73.2 us
  Pallas kernels  64.6 us (88%)
  local copies, waits for them, and re-layouts  5.53 us (8%)
  between operations  3.06 us (4%)
    pallas_call x1, Pallas kernels, per_device(): pl.pallas_call(kernel, out_shape=(jax.ShapeDtypeStruct(concentration.shap...  64.6 us
    unnamed x11, local copies, waits for them, and re-layouts  5.53 us

commit v1 on v0

--- a/solution.py
+++ b/solution.py
@@ -57,14 +57,15 @@
 def make_kernel(zl, yl, ng, ny, factor):
     nv = yl // 8
     yr = yl + 2 * R
-    g1 = 4 if ng % 4 == 0 else 1
-    size1 = g1 * ny
-    size2 = ng // g1
+    n_core = 2 if ny % 2 == 0 else 1
+    n_z = 8 if ng % 8 == 0 else 1
+    size1 = n_core * n_z
+    size2 = (ny // n_core) * (ng // n_z)
 
     def kernel(
         conc, cot, w_in, b_in, w_out, b_out,
-        out, out_wi, out_bi, out_wo, out_bo,
-        C, A0, MU1, M1, SG1, C2, MU2, M2, SG2, RR, UU, VV, A1, H1, H2,
+        out, out_sums,
+        C, A0, MU1, M1, SG1, C2, MU2, M2, SG2, RR, UU, VV, A1, GS, H1, H2,
         WL, WOF, CT, UB, PACC, TACC, GACC, OUTV, RED, RED2, MSG, MSG2,
         send_sem, recv_sem, local_sem, rs_send, rs_recv, rs2_send, rs2_recv,
     ):
@@ -74,17 +75,17 @@
         def neighbour(dz, dy):
             return (lax.rem(gz + dz + ng, ng), lax.rem(gy + dy + ny, ny))
 
-        block1 = gz // g1
-        place1 = lax.rem(gz, g1) * ny + gy
-        place2 = block1
+        place1 = lax.rem(gy, n_core) * n_z + lax.rem(gz, n_z)
+        place2 = (gy // n_core) * (ng // n_z) + gz // n_z
 
         def peer1(k):
             q = lax.rem(place1 + k, size1)
-            return q, (block1 * g1 + q // ny, lax.rem(q, ny))
+            return q, (gz // n_z * n_z + lax.rem(q, n_z), gy // n_core * n_core + q // n_z)
 
         def peer2(k):
             q = lax.rem(place2 + k, size2)
-            return q, (q * g1 + lax.rem(gz, g1), gy)
+            outer = ng // n_z
+            return q, (lax.rem(q, outer) * n_z + lax.rem(gz, n_z), q // outer * n_core + lax.rem(gy, n_core))
 
         local_c = pltpu.make_async_copy(
             conc, C.at[pl.ds(WC, zl), pl.ds(R, yl)], local_sem.at[0])
@@ -121,25 +122,23 @@
             return pl.ds(0, yl), pl.ds(R, yl)
 
         def halo(which, source, field, width):
-            copies = []
+            copies = {}
             for n, (dz, dy) in enumerate(DIRECTIONS):
                 sz, tz = span_z(dz, width)
                 sy, ty = span_y(dy)
-                copies.append(pltpu.make_async_remote_copy(
+                copies[dz, dy] = pltpu.make_async_remote_copy(
                     src_ref=source.at[sz, sy],
                     dst_ref=field.at[tz, ty],
                     send_sem=send_sem.at[which, n],
                     recv_sem=recv_sem.at[which, n],
                     device_id=neighbour(dz, dy),
                     device_id_type=MESH,
-                ))
+                )
             return copies
 
         halo_c = halo(0, conc, C, WC)
         halo_a = halo(1, cot, A0, WA)
-        for copy in halo_c:
-            copy.start()
-        for copy in halo_a:
+        for copy in [*halo_c.values(), *halo_a.values()]:
             copy.start()
 
         lane = iota((UNITS, 128), 1)
@@ -148,7 +147,8 @@
         wo_col = jnp.sum(jnp.where(eye, w_out[...], 0.0), axis=1, keepdims=True)
         packed = jnp.where(lane == 4, bi_col, jnp.where(lane == 5, wo_col, 0.0))
         for k in range(4):
-            packed = jnp.where(lane == k, w_in[:, k:k + 1], packed)
+            w_col = jnp.sum(jnp.where(eye, w_in[k:k + 1, :], 0.0), axis=1, keepdims=True)
+            packed = jnp.where(lane == k, w_col, packed)
         spread = (iota((ROWS, UNITS), 0) // 8 == iota((ROWS, UNITS), 1)).astype(F32)
         params = dot(spread, packed, HIGH)
         row = iota((ROWS, 128), 0)
@@ -211,9 +211,8 @@
             e = jnp.exp(s)
             return jnp.log(1.0 + e) + FLOOR, e / (1.0 + e)
 
-        def forward_one(p):
-            for d in range(2):
-                q = p + d
+        def forward_one(planes):
+            for q in planes:
                 c, lap, sq, _ = fields_of(C, q)
                 mu = c * c * c - c - KAPPA * lap
                 MU1[q] = mu
@@ -234,22 +233,26 @@
                         M1[q, rows] = m[:, 128 * i:128 * i + 128]
                         SG1[q, rows] = sg[:, 128 * i:128 * i + 128]
 
-        def loop(first, last, body, step=2):
-            def run(i, carry):
-                body(first + step * i)
-                return carry
-            lax.fori_loop(0, (last - first) // step, run, 0)
-
-        local_c.wait()
-        for n in range(2):
-            halo_c[n].wait_recv()
-        loop(WC + 2, WC + zl - 2, forward_one)
-        for n in range(2, 8):
-            halo_c[n].wait_recv()
-        loop(1, WC + 2, forward_one)
-        loop(WC + zl - 2, 2 * WC + zl - 1, forward_one)
-
-        def advance(p):
+        def wait_for(copies, sides):
+            for dz, dy in DIRECTIONS:
+                if (dz == 0) == (sides == "y"):
+                    copies[dz, dy].wait_recv()
+
+        low, high = WC, WC + zl - 1
+
+        def inner(width, body):
+            for p in range(low + width, high - width, 2):
+                body((p, p + 1))
+
+        def outer(first, last, body):
+            for k in range(-first, last):
+                body((low - 1 - k, high + 1 + k))
+
+        def advance(planes):
+            for p in planes:
+                advance_plane(p)
+
+        def advance_plane(p):
             mu, m = MU1[p], M1[p]
             def face(mu_a, m_a, mu_b, m_b):
                 return (m_a + m_b) * (mu_b - mu_a)
@@ -260,12 +263,9 @@
             total = (up - down) + (fy - ym(fy)) + (fx - xm(fx))
             C2[p] = C[p] + (0.5 * STEP) * total
 
-        loop(2, 2 * WC + zl - 2, advance, 1)
-
-        def forward_two(p):
+        def forward_two(planes):
             feats = []
-            for d in range(2):
-                q = p + d
+            for q in planes:
                 c, lap, sq, _ = fields_of(C2, q)
                 mu = c * c * c - c - KAPPA * lap
                 MU2[q] = mu
@@ -275,112 +275,133 @@
                 h = units([[f[a] for f in feats[d]] for d, a in places])
                 m, sg = soft(score(h))
                 for i, (d, a) in enumerate(places):
-                    q = p + d
+                    q = planes[d]
                     H2[q, a] = h[:, 128 * i:128 * i + 128]
                     mi, si = m[:, 128 * i:128 * i + 128], sg[:, 128 * i:128 * i + 128]
                     for start in ([R + 8 * a] if a < nv else [0, R + yl]):
                         M2[q, pl.ds(start, 8)] = mi
                         SG2[q, pl.ds(start, 8)] = si
 
-        loop(3, 2 * WC + zl - 3, forward_two)
-
-        def backward(p, adj, shift, c_ref, mu_ref, m_ref, sg_ref, h_ref):
-            states = []
-            for q in p:
-                c, lap, sq, slopes = fields_of(c_ref, q)
-                mu, m, a = mu_ref[q], m_ref[q], adj[q + shift]
-                def faces(mu_a, m_a, a_a, mu_b, m_b, a_b):
-                    da = a_b - a_a
-                    return (mu_b - mu_a) * da, (m_a + m_b) * da
-                q_up, r_up = faces(mu, m, a, mu_ref[q + 1], m_ref[q + 1], adj[q + 1 + shift])
-                q_dn, r_dn = faces(mu_ref[q - 1], m_ref[q - 1], adj[q - 1 + shift], mu, m, a)
-                q_y, r_y = faces(mu, m, a, yp(mu), yp(m), yp(a))
-                q_x, r_x = faces(mu, m, a, xp(mu), xp(m), xp(a))
-                adj_mob = (q_up + q_dn) + (q_y + ym(q_y)) + (q_x + xm(q_x))
-                adj_pot = (r_up - r_dn) + (r_y - ym(r_y)) + (r_x - xm(r_x))
-                g = (-0.5 * STEP) * adj_mob * sg_ref[q]
-                adj_pot = (0.5 * STEP) * adj_pot
-                states.append(dict(c=c, a=a, slopes=slopes, adj_pot=adj_pot, g=pack(g), f=[pack(f) for f in (c, lap, sq, mu)], A={}))
-
-            work = [((d, b), (d, b + 1)) for d in range(2) for b in range(0, nv, 2)] + [((0, nv), (1, nv))]
+        def faces(field, adj, shift, q, of):
+            v, a = field[q], adj[q + shift]
+            up = of(v, field[q + 1], adj[q + 1 + shift] - a)
+            down = of(field[q - 1], v, a - adj[q - 1 + shift])
+            fy = of(v, yp(v), yp(a) - a)
+            fx = of(v, xp(v), xp(a) - a)
+            return (up, down), (fy, ym(fy)), (fx, xm(fx))
+
+        def score_adjoint(q, adj, shift, mu_ref, sg_ref):
+            z, y, x = faces(mu_ref, adj, shift, q, lambda here, there, da: (there - here) * da)
+            adj_mob = (z[0] + z[1]) + (y[0] + y[1]) + (x[0] + x[1])
+            return (-0.5 * STEP) * adj_mob * sg_ref[q]
+
+        def flux_adjoint(q, adj, shift, m_ref):
+            z, y, x = faces(m_ref, adj, shift, q, lambda here, there, da: (here + there) * da)
+            return (0.5 * STEP) * ((z[0] - z[1]) + (y[0] - y[1]) + (x[0] - x[1]))
+
+        def places_of(with_core, with_sides):
+            core = [((d, b), (d, b + 1)) for d in range(2) for b in range(0, nv, 2)] if with_core else []
+            return core + ([((0, nv), (1, nv))] if with_sides else [])
+
+        def hidden(planes, places, h_ref):
+            h = jnp.concatenate([h_ref[planes[d], b] for d, b in places], axis=1)
+            return 1.0 - h * h
+
+        def sums(planes, g, c_ref, mu_ref, h_ref, ub):
+            feats = []
+            for q in planes:
+                c, lap, sq, _ = fields_of(c_ref, q)
+                feats.append([pack(f) for f in (c, lap, sq, mu_ref[q])])
             gg = []
-            for n, places in enumerate(work):
-                h = jnp.concatenate([h_ref[p[d], b] for d, b in places], axis=1)
-                u = 1.0 - h * h
-                u_high = u.astype(BF16)
-                back = dot(CT[...], u_high)
-                back = back[:32] + back[32:]
-                g = jnp.concatenate([states[d]["g"][b] for d, b in places], axis=1)
-                for i, (d, b) in enumerate(places):
-                    states[d]["A"][b] = [
-                        back[8 * k:8 * k + 8, 128 * i:128 * i + 128] * states[d]["g"][b] for k in range(4)
-                    ]
-                if n < len(work) - 1:
-                    UB[pl.ds(0, ROWS), pl.ds(256 * n, 256)] = u_high
-                    UB[pl.ds(ROWS, ROWS), pl.ds(256 * n, 256)] = (u - u_high.astype(F32)).astype(BF16)
-                    feats = [jnp.concatenate([states[d]["f"][k][b] for d, b in places], axis=1) for k in range(4)]
-                    stack = jnp.concatenate([g * f for f in feats] + [g, jnp.zeros((8, 256), F32)], axis=0)
-                    s_high, s_low = split(stack)
-                    gg.append(jnp.concatenate([s_high, s_low, jnp.zeros((32, 256), BF16)], axis=0))
-            return states, gg
-
-        def sums(p, states, gg, h_ref):
-            rhs = jnp.concatenate(gg, axis=1)
+            for n, places in enumerate(places_of(True, False)):
+                u = hidden(planes, places, h_ref)
+                u_high, u_low = split(u)
+                ub[pl.ds(0, ROWS), pl.ds(256 * n, 256)] = u_high
+                ub[pl.ds(ROWS, ROWS), pl.ds(256 * n, 256)] = u_low
+                gs = jnp.concatenate([g[d][b] for d, b in places], axis=1)
+                stack = [gs * jnp.concatenate([feats[d][k][b] for d, b in places], axis=1) for k in range(4)]
+                s_high, s_low = split(jnp.concatenate(stack + [gs, jnp.zeros((8, 256), F32)], axis=0))
+                gg.append(jnp.concatenate([s_high, s_low, jnp.zeros((32, 256), BF16)], axis=0))
             PACC[...] += lax.dot_general(
-                UB[...], rhs, (((1,), (1,)), ((), ())), preferred_element_type=F32)
+                ub[...], jnp.concatenate(gg, axis=1), (((1,), (1,)), ((), ())), preferred_element_type=F32)
             total = TACC[...].reshape(UNITS, 8, 128)
             g_total = GACC[...]
             for d in range(2):
                 for b in range(nv):
-                    g = states[d]["g"][b]
-                    total = total + h_ref[p[d], b].reshape(UNITS, 8, 128) * g[None]
-                    g_total = g_total + g
+                    total = total + h_ref[planes[d], b].reshape(UNITS, 8, 128) * g[d][b][None]
+                    g_total = g_total + g[d][b]
             TACC[...] = total.reshape(ROWS, 128)
             GACC[...] = g_total
 
-        def finish(p, states):
-            for d in range(2):
-                s = states[d]
-                A = [unpack([s["A"][b][k] for b in range(nv + 1)]) for k in range(4)]
-                adj_pot = s["adj_pot"] + A[3]
-                adj_lap = A[1] - KAPPA * adj_pot
-                zed, why, ex = (A[2] * slope for slope in s["slopes"])
-                rest = s["a"] + A[0] + (3.0 * s["c"] * s["c"] - 1.0) * adj_pot - 6.0 * adj_lap
+        def finish(planes, g, adj, shift, c_ref, m_ref, h_ref):
+            A = [[None] * (nv + 1) for _ in planes]
+            for places in places_of(True, True):
+                back = dot(CT[...], hidden(planes, places, h_ref).astype(BF16))
+                back = back[:32] + back[32:]
+                for i, (d, b) in enumerate(places):
+                    A[d][b] = [back[8 * k:8 * k + 8, 128 * i:128 * i + 128] * g[d][b] for k in range(4)]
+            for d, q in enumerate(planes):
+                a_c, a_lap, a_sq, a_mu = (unpack([A[d][b][k] for b in range(nv + 1)]) for k in range(4))
+                c, _, _, slopes = fields_of(c_ref, q)
+                adj_pot = flux_adjoint(q, adj, shift, m_ref) + a_mu
+                adj_lap = a_lap - KAPPA * adj_pot
+                zed, why, ex = (a_sq * slope for slope in slopes)
+                rest = adj[q + shift] + a_c + (3.0 * c * c - 1.0) * adj_pot - 6.0 * adj_lap
                 rest = rest + (xm(adj_lap + ex) + xp(adj_lap - ex)) + (ym(adj_lap + why) + yp(adj_lap - why))
-                RR[p[d]] = rest
-                UU[p[d]] = adj_lap + zed
-                VV[p[d]] = adj_lap - zed
-
-        for copy in halo_a:
-            copy.wait_recv()
-        local_a.wait()
+                RR[q] = rest
+                UU[q] = adj_lap + zed
+                VV[q] = adj_lap - zed
+
+        turn = [0]
+
+        def buffer():
+            turn[0] ^= 1
+            return UB.at[turn[0]]
 
         def back_two(with_sums):
-            def body(p):
-                states, gg = backward(p, A0, WA - WC, C2, MU2, M2, SG2, H2)
+            def body(planes):
+                g = [pack(score_adjoint(q, A0, WA - WC, MU2, SG2)) for q in planes]
                 if with_sums:
-                    sums(p, states, gg, H2)
-                finish(p, states)
+                    sums(planes, g, C2, MU2, H2, buffer())
+                finish(planes, g, A0, WA - WC, C2, M2, H2)
             return body
 
-        def back_one(with_sums):
-            def body(p):
-                states, gg = backward(p, A1, 0, C, MU1, M1, SG1, H1)
-                if with_sums:
-                    sums(p, states, gg, H1)
-                finish(p, states)
-            return body
-
-        loop(0, 3, lambda k: back_two(False)((WC - 1 - k, WC + zl + k)), 1)
-        loop(WC, WC + zl, lambda p: back_two(True)((p, p + 1)))
+        def back_one_sums(planes):
+            g = [pack(score_adjoint(q, A1, 0, MU1, SG1)) for q in planes]
+            sums(planes, g, C, MU1, H1, buffer())
+            for d, q in enumerate(planes):
+                for b in range(nv + 1):
+                    GS[q, pl.ds(8 * b, 8)] = g[d][b]
+
+        def back_one_rest(planes):
+            g = [[GS[q, pl.ds(8 * b, 8)] for b in range(nv + 1)] for q in planes]
+            finish(planes, g, A1, 0, C, M1, H1)
+
+        def back_one_sides(planes):
+            g = [pack(score_adjoint(q, A1, 0, MU1, SG1)) for q in planes]
+            finish(planes, g, A1, 0, C, M1, H1)
 
         def join(p):
             A1[p] = RR[p] + UU[p - 1] + VV[p + 1]
 
-        loop(WC - 2, WC + zl + 2, join, 1)
-
-        loop(WC, WC + zl, lambda p: back_one(True)((p, p + 1)))
-        back_one(False)((WC - 1, WC + zl))
+        local_c.wait()
+        wait_for(halo_c, "y")
+        inner(1, forward_one)
+        inner(2, advance)
+        inner(3, forward_two)
+        local_a.wait()
+        wait_for(halo_a, "y")
+        inner(4, back_two(True))
+        wait_for(halo_c, "z")
+        outer(1, 6, forward_one)
+        outer(2, 5, advance)
+        outer(3, 4, forward_two)
+        wait_for(halo_a, "z")
+        outer(4, 0, back_two(True))
+        outer(0, 3, back_two(False))
+        for p in range(low - 2, high + 3):
+            join(p)
+        inner(0, back_one_sums)
 
         both = PACC[pl.ds(0, ROWS)] + PACC[pl.ds(ROWS, ROWS)]
         both = jnp.where(same & (col < 96), both, 0.0)
@@ -396,10 +417,8 @@
         first_row = iota((UNITS, 128), 0) == 0
         grads = jnp.where(lane == 5, t_col, grads)
         grads = jnp.where((lane == 6) & first_row, g_sum, grads)
-        message = grads[0:8]
-        for n in range(1, 4):
-            message = message + pltpu.roll(grads[8 * n:8 * n + 8], 32 * n, 1)
-        MSG[...] = message
+        square = jnp.concatenate([grads, jnp.zeros((128 - UNITS, 128), F32)], axis=0)
+        MSG[...] = square.T[0:8]
 
         def exchange(size, place, peer, src, slots, s_sem, r_sem):
             copies = []
@@ -426,11 +445,11 @@
 
         sent1 = exchange(size1, place1, peer1, MSG, RED, rs_send, rs_recv)
 
-        def result(p):
+        outer(0, 1, back_one_sides)
+        inner(0, back_one_rest)
+        for p in range(low, high + 1):
             rows = pl.ds(R, yl)
             OUTV[p - WC] = RR[p, rows] + UU[p - 1, rows] + VV[p + 1, rows]
-
-        loop(WC, WC + zl, result, 1)
         write = pltpu.make_async_copy(OUTV, out, local_sem.at[2])
         write.start()
 
@@ -441,18 +460,23 @@
             total = collected(size2, peer2, sent2, MSG2, RED2, rs2_send, rs2_recv)
         else:
             sent2 = []
-        total = total * factor
-        full = jnp.concatenate([total] + [pltpu.roll(total, 128 - 32 * n, 1) for n in range(1, 4)], axis=0)
-        out_wi[...] = full[:, 0:4]
-        out_bi[...] = jnp.sum(jnp.where(eye, full[:, 4:5], 0.0), axis=0, keepdims=True)
-        out_wo[...] = jnp.sum(jnp.where(eye, full[:, 5:6], 0.0), axis=0, keepdims=True)
-        out_bo[...] = full[0:1, 6:7]
-
-        for copy in halo_c + halo_a + sent1 + sent2:
+        out_sums[...] = total * factor
+
+        for copy in [*halo_c.values(), *halo_a.values(), *sent1, *sent2]:
             copy.wait_send()
         write.wait()
 
     return kernel, yr, size1, size2
+
+
+def hand_over(field, sums, out, out_wi, out_bi, out_wo, out_bo, sem):
+    copy = pltpu.make_async_copy(field, out, sem)
+    copy.start()
+    out_wi[...] = sums[0:4, 0:UNITS]
+    out_bi[...] = sums[4:5, 0:UNITS]
+    out_wo[...] = sums[5:6, 0:UNITS]
+    out_bo[...] = sums[6:7, 0:1]
+    copy.wait()
 
 
 def per_device(ng, ny, concentration, cotangent, w_in, b_in, w_out, b_out):
@@ -469,25 +493,23 @@
         kernel,
         out_shape=(
             jax.ShapeDtypeStruct(concentration.shape, F32),
-            jax.ShapeDtypeStruct((UNITS, 4), F32),
-            jax.ShapeDtypeStruct((1, UNITS), F32),
-            jax.ShapeDtypeStruct((1, UNITS), F32),
-            jax.ShapeDtypeStruct((1, 1), F32),
+            jax.ShapeDtypeStruct((8, 128), F32),
         ),
         in_specs=[anywhere, anywhere, vmem, vmem, vmem, smem],
-        out_specs=(anywhere, vmem, vmem, vmem, vmem),
+        out_specs=(anywhere, vmem),
         scratch_shapes=[
             field,
             pltpu.VMEM((zl + 2 * WA, yr, nx), F32),
             field, field, field,
             field, field, field, field,
             field, field, field, field,
+            pltpu.VMEM((planes, yl + 8, nx), F32),
             pltpu.VMEM((planes, nv + 1, ROWS, nx), F32),
             pltpu.VMEM((planes, nv + 1, ROWS, nx), F32),
             pltpu.VMEM((ROWS, 128), BF16),
             pltpu.VMEM((ROWS, 128), F32),
             pltpu.VMEM((64, ROWS), BF16),
-            pltpu.VMEM((2 * ROWS, 2 * yl // 8 * 128), BF16),
+            pltpu.VMEM((2, 2 * ROWS, 2 * yl // 8 * 128), BF16),
             pltpu.VMEM((2 * ROWS, 128), F32),
             pltpu.VMEM((ROWS, 128), F32),
             pltpu.VMEM((8, 128), F32),
@@ -508,9 +530,22 @@
             collective_id=0, has_side_effects=True, vmem_limit_bytes=60 * 1024 * 1024
         ),
     )(
-        concentration, cotangent, w_in, b_in.reshape(1, UNITS), w_out.reshape(1, UNITS), b_out.reshape(1, 1)
+        concentration, cotangent, w_in.T, b_in.reshape(1, UNITS), w_out.reshape(1, UNITS), b_out.reshape(1, 1)
     )
-    return (outs[0], outs[1], outs[2].reshape(UNITS), outs[3].reshape(UNITS), outs[4].reshape(()))
+    outs = pl.pallas_call(
+        hand_over,
+        out_shape=(
+            jax.ShapeDtypeStruct(concentration.shape, F32),
+            jax.ShapeDtypeStruct((4, UNITS), F32),
+            jax.ShapeDtypeStruct((1, UNITS), F32),
+            jax.ShapeDtypeStruct((1, UNITS), F32),
+            jax.ShapeDtypeStruct((1, 1), F32),
+        ),
+        in_specs=[anywhere, vmem],
+        out_specs=(anywhere, vmem, vmem, vmem, vmem),
+        scratch_shapes=[pltpu.SemaphoreType.DMA],
+    )(*outs)
+    return (outs[0], outs[1].T, outs[2].reshape(UNITS), outs[3].reshape(UNITS), outs[4].reshape(()))
 
 
 def solution(mesh):

time: 73.4 us -> 58.6 us (0.80)
  Pallas kernels: 64.6 us -> 56.9 us
  local copies, waits for them, and re-layouts: 5.53 us -> 0 us
  between operations: 3.06 us -> 1.45 us
    pallas_call x1, Pallas kernels: 64.6 us -> 46.6 us  [per_device(): pl.pallas_call(kernel, out_shape=(jax.ShapeDtypeStruct(concentration.shap...]
    pallas_call x0 -> x1, Pallas kernels: none -> 10.3 us  [per_device(): pl.pallas_call(hand_over, out_shape=(jax.ShapeDtypeStruct(concentration.s...]
    unnamed x11 -> x0, local copies, waits for them, and re-layouts: 5.53 us -> none
where the time goes in v1:
time: 58.6 us; the launch traced here: 58.4 us
  Pallas kernels  56.9 us (97%)
  between operations  1.45 us (2%)
    pallas_call x1, Pallas kernels, per_device(): pl.pallas_call(kernel, out_shape=(jax.ShapeDtypeStruct(concentration.shap...  46.6 us
    pallas_call x1, Pallas kernels, per_device(): pl.pallas_call(hand_over, out_shape=(jax.ShapeDtypeStruct(concentration.s...  10.3 us

profile of v1, /device:TPU:1, one launch (start us, length us, event | category | flops | bytes accessed | tf_op | source)
XLA Modules:
  0.0 58.4 jit_solution(8118378817644100360)
XLA Ops:
  1.3 46.6 %shard_map.101 = (f32[16,32,128]{2,1,0:T(8,128)}, f32[8,128]{1,0:T(8,128)}) custom-call(f32[16,32,128]{2,1,0:T(8,128)} %conc.1, f32[16,32,128]{2,1,0:T(8,128)} %cot.1, f32[4,32]{1,0:T(4,128)} %bitcast.9, f32[1,32]{1,0:T(1,128)} %bitcast.10, f32[1,32]{1,0:T(1,128)} %bitcast.11, f32[1,1]{1,0:T(1,128)} %bitcast.8.b_out), custom_call_target="tpu_custom_call" | custom-call | tf_op jit(solution)/shard_map/pallas_call | solution.py:492
  47.9 10.3 %shard_map.102 = (f32[16,32,128]{2,1,0:T(8,128)}, f32[4,32]{1,0:T(4,128)}, f32[1,32]{1,0:T(1,128)}, f32[1,32]{1,0:T(1,128)}, f32[1,1]{1,0:T(1,128)}) custom-call(f32[16,32,128]{2,1,0:T(8,128)} %get-tuple-element.12.field, f32[8,128]{1,0:T(8,128)} %get-tuple-element.13.sums), custom_call_target="tpu_custom_call" | custom-call | tf_op jit(solution)/shard_map/pallas_call | solution.py:535

commit v2 on v1

--- a/solution.py
+++ b/solution.py
@@ -23,6 +23,11 @@
 
 
 DIRECTIONS = [(dz, dy) for dz in (0, -1, 1) for dy in (-1, 1, 0) if (dz, dy) != (0, 0)]
+
+CORNER_C = ((0, 2, 8), (2, 4, 4))
+CORNER_A = ((0, 3, 4),)
+PIECES_C = [(dz, dy, n) for dz, dy in DIRECTIONS for n in range(len(CORNER_C) if dz * dy else 1)]
+PIECES_A = [(dz, dy, n) for dz, dy in DIRECTIONS for n in range(len(CORNER_A) if dz * dy else 1)]
 
 
 def iota(shape, dim):
@@ -93,6 +98,17 @@
             cot, A0.at[pl.ds(WA, zl), pl.ds(R, yl)], local_sem.at[1])
         local_c.start()
         local_a.start()
+
+        for margin in (0, R + yl):
+            for first, length in ((0, WC - 2), (WC + zl + 2, WC - 2)):
+                rows = pl.ds(margin + (0 if margin == 0 else 4), 4)
+                C[pl.ds(first, length), rows] = jnp.zeros((length, 4, 128), F32)
+            for p in (0, 2 * WC + zl - 1):
+                C[p, pl.ds(margin, R)] = jnp.zeros((R, 128), F32)
+            rows = pl.ds(margin + (0 if margin == 0 else 4), 4)
+            A0[:, rows] = jnp.zeros((zl + 2 * WA, 4, 128), F32)
+            for p in (0, 2 * WA + zl - 1):
+                A0[p, pl.ds(margin, R)] = jnp.zeros((R, 128), F32)
 
         barrier = pltpu.get_barrier_semaphore()
         count = 0
@@ -107,26 +123,20 @@
             count += 1
         pl.semaphore_wait(barrier, count)
 
-        def span_z(dz, width):
-            if dz > 0:
-                return pl.ds(zl - width, width), pl.ds(0, width)
-            if dz < 0:
-                return pl.ds(0, width), pl.ds(width + zl, width)
-            return pl.ds(0, zl), pl.ds(width, zl)
-
-        def span_y(dy):
-            if dy > 0:
-                return pl.ds(yl - R, R), pl.ds(0, R)
-            if dy < 0:
-                return pl.ds(0, R), pl.ds(R + yl, R)
-            return pl.ds(0, yl), pl.ds(R, yl)
-
-        def halo(which, source, field, width):
+        def span(d, size, edge, first, length):
+            if d > 0:
+                return pl.ds(size - first - length, length), pl.ds(edge - first - length, length)
+            if d < 0:
+                return pl.ds(first, length), pl.ds(edge + size + first, length)
+            return pl.ds(0, size), pl.ds(edge, size)
+
+        def halo(which, source, field, pieces, width, rows, corner):
             copies = {}
-            for n, (dz, dy) in enumerate(DIRECTIONS):
-                sz, tz = span_z(dz, width)
-                sy, ty = span_y(dy)
-                copies[dz, dy] = pltpu.make_async_remote_copy(
+            for n, (dz, dy, part) in enumerate(pieces):
+                first, planes, high_rows = corner[part] if dz * dy else (0, width, rows)
+                sz, tz = span(dz, zl, width, first, planes)
+                sy, ty = span(dy, yl, R, 0, high_rows)
+                copies[dz, dy, part] = pltpu.make_async_remote_copy(
                     src_ref=source.at[sz, sy],
                     dst_ref=field.at[tz, ty],
                     send_sem=send_sem.at[which, n],
@@ -136,10 +146,12 @@
                 )
             return copies
 
-        halo_c = halo(0, conc, C, WC)
-        halo_a = halo(1, cot, A0, WA)
-        for copy in [*halo_c.values(), *halo_a.values()]:
+        halo_c = halo(0, conc, C, PIECES_C, WC, 8, CORNER_C)
+        halo_a = halo(1, cot, A0, PIECES_A, WA, 4, CORNER_A)
+        for copy in halo_c.values():
             copy.start()
+        for dy in (-1, 1):
+            halo_a[0, dy, 0].start()
 
         lane = iota((UNITS, 128), 1)
         eye = iota((UNITS, UNITS), 0) == iota((UNITS, UNITS), 1)
@@ -186,9 +198,9 @@
         def unpack(blocks):
             return jnp.concatenate([blocks[-1]] + blocks[:-1] + [blocks[-1]], axis=0)
 
-        def fields_of(c_ref, p):
-            c = c_ref[p]
-            zu, zd = c_ref[p + 1], c_ref[p - 1]
+        def fields_of(c_ref, p, rows=slice(None)):
+            c = c_ref[p, rows]
+            zu, zd = c_ref[p + 1, rows], c_ref[p - 1, rows]
             yu, yd = yp(c), ym(c)
             xu, xd = xp(c), xm(c)
             lap = ((zu + zd) + (yu + yd)) + (xu + xd) - 6.0 * c
@@ -211,32 +223,44 @@
             e = jnp.exp(s)
             return jnp.log(1.0 + e) + FLOOR, e / (1.0 + e)
 
-        def forward_one(planes):
+        def forward_blocks(q, feats, ids, offset):
+            pair = [[f[8 * i - offset:8 * i - offset + 8] for f in feats] for i in ids]
+            h = units(pair)
+            if ids[0] > nv:
+                mask = (iota((ROWS, 128), 0) & 7) < 4
+                H1[q, nv] = jnp.where(mask, h[:, :128], h[:, 128:])
+            else:
+                for i in range(2):
+                    H1[q, ids[i] - 1] = h[:, 128 * i:128 * i + 128]
+            m, sg = soft(score(h))
+            for i in range(2):
+                rows = pl.ds(8 * ids[i], 8)
+                M1[q, rows] = m[:, 128 * i:128 * i + 128]
+                SG1[q, rows] = sg[:, 128 * i:128 * i + 128]
+
+        def forward_one_early(planes):
+            for q in planes:
+                c, lap, sq, _ = fields_of(C, q, pl.ds(R, yl))
+                feats = [c, lap, sq, c * c * c - c - KAPPA * lap]
+                for i in range(2, nv, 2):
+                    forward_blocks(q, feats, (i, i + 1), R)
+
+        def forward_one(planes, early=False):
             for q in planes:
                 c, lap, sq, _ = fields_of(C, q)
                 mu = c * c * c - c - KAPPA * lap
                 MU1[q] = mu
                 feats = [c, lap, sq, mu]
-                for a in range(0, nv + 2, 2):
-                    ids = [1 + a, 2 + a] if a < nv else [nv + 1, 0]
-                    pair = [[f[8 * i:8 * i + 8] for f in feats] for i in ids]
-                    h = units(pair)
-                    if a < nv:
-                        H1[q, a] = h[:, :128]
-                        H1[q, a + 1] = h[:, 128:]
-                    else:
-                        mask = (iota((ROWS, 128), 0) & 7) < 4
-                        H1[q, nv] = jnp.where(mask, h[:, :128], h[:, 128:])
-                    m, sg = soft(score(h))
-                    for i in range(2):
-                        rows = pl.ds(8 * ids[i], 8)
-                        M1[q, rows] = m[:, 128 * i:128 * i + 128]
-                        SG1[q, rows] = sg[:, 128 * i:128 * i + 128]
+                if not early:
+                    for i in range(2, nv, 2):
+                        forward_blocks(q, feats, (i, i + 1), 0)
+                forward_blocks(q, feats, (1, nv), 0)
+                forward_blocks(q, feats, (nv + 1, 0), 0)
 
         def wait_for(copies, sides):
-            for dz, dy in DIRECTIONS:
+            for dz, dy, part in copies:
                 if (dz == 0) == (sides == "y"):
-                    copies[dz, dy].wait_recv()
+                    copies[dz, dy, part].wait_recv()
 
         low, high = WC, WC + zl - 1
 
@@ -282,21 +306,25 @@
                         M2[q, pl.ds(start, 8)] = mi
                         SG2[q, pl.ds(start, 8)] = si
 
-        def faces(field, adj, shift, q, of):
-            v, a = field[q], adj[q + shift]
-            up = of(v, field[q + 1], adj[q + 1 + shift] - a)
-            down = of(field[q - 1], v, a - adj[q - 1 + shift])
-            fy = of(v, yp(v), yp(a) - a)
-            fx = of(v, xp(v), xp(a) - a)
+        def jumps(q, adj, shift):
+            a = adj[q + shift]
+            return adj[q + 1 + shift] - a, a - adj[q - 1 + shift], yp(a) - a, xp(a) - a
+
+        def faces(field, q, da, of):
+            v = field[q]
+            up = of(v, field[q + 1], da[0])
+            down = of(field[q - 1], v, da[1])
+            fy = of(v, yp(v), da[2])
+            fx = of(v, xp(v), da[3])
             return (up, down), (fy, ym(fy)), (fx, xm(fx))
 
-        def score_adjoint(q, adj, shift, mu_ref, sg_ref):
-            z, y, x = faces(mu_ref, adj, shift, q, lambda here, there, da: (there - here) * da)
+        def score_adjoint(q, da, mu_ref, sg_ref):
+            z, y, x = faces(mu_ref, q, da, lambda here, there, d: (there - here) * d)
             adj_mob = (z[0] + z[1]) + (y[0] + y[1]) + (x[0] + x[1])
             return (-0.5 * STEP) * adj_mob * sg_ref[q]
 
-        def flux_adjoint(q, adj, shift, m_ref):
-            z, y, x = faces(m_ref, adj, shift, q, lambda here, there, da: (here + there) * da)
+        def flux_adjoint(q, da, m_ref):
+            z, y, x = faces(m_ref, q, da, lambda here, there, d: (here + there) * d)
             return (0.5 * STEP) * ((z[0] - z[1]) + (y[0] - y[1]) + (x[0] - x[1]))
 
         def places_of(with_core, with_sides):
@@ -307,10 +335,9 @@
             h = jnp.concatenate([h_ref[planes[d], b] for d, b in places], axis=1)
             return 1.0 - h * h
 
-        def sums(planes, g, c_ref, mu_ref, h_ref, ub):
+        def sums(planes, g, local, mu_ref, h_ref, ub):
             feats = []
-            for q in planes:
-                c, lap, sq, _ = fields_of(c_ref, q)
+            for q, (c, lap, sq, _) in zip(planes, local):
                 feats.append([pack(f) for f in (c, lap, sq, mu_ref[q])])
             gg = []
             for n, places in enumerate(places_of(True, False)):
@@ -333,7 +360,7 @@
             TACC[...] = total.reshape(ROWS, 128)
             GACC[...] = g_total
 
-        def finish(planes, g, adj, shift, c_ref, m_ref, h_ref):
+        def finish(planes, g, steps, local, adj, shift, m_ref, h_ref):
             A = [[None] * (nv + 1) for _ in planes]
             for places in places_of(True, True):
                 back = dot(CT[...], hidden(planes, places, h_ref).astype(BF16))
@@ -342,8 +369,8 @@
                     A[d][b] = [back[8 * k:8 * k + 8, 128 * i:128 * i + 128] * g[d][b] for k in range(4)]
             for d, q in enumerate(planes):
                 a_c, a_lap, a_sq, a_mu = (unpack([A[d][b][k] for b in range(nv + 1)]) for k in range(4))
-                c, _, _, slopes = fields_of(c_ref, q)
-                adj_pot = flux_adjoint(q, adj, shift, m_ref) + a_mu
+                c, _, _, slopes = local[d]
+                adj_pot = flux_adjoint(q, steps[d], m_ref) + a_mu
                 adj_lap = a_lap - KAPPA * adj_pot
                 zed, why, ex = (a_sq * slope for slope in slopes)
                 rest = adj[q + shift] + a_c + (3.0 * c * c - 1.0) * adj_pot - 6.0 * adj_lap
@@ -358,39 +385,51 @@
             turn[0] ^= 1
             return UB.at[turn[0]]
 
+        def start_of(planes, adj, shift, c_ref):
+            return [jumps(q, adj, shift) for q in planes], [fields_of(c_ref, q) for q in planes]
+
         def back_two(with_sums):
             def body(planes):
-                g = [pack(score_adjoint(q, A0, WA - WC, MU2, SG2)) for q in planes]
+                shift = WA - WC
+                steps, local = start_of(planes, A0, shift, C2)
+                g = [pack(score_adjoint(q, da, MU2, SG2)) for q, da in zip(planes, steps)]
                 if with_sums:
-                    sums(planes, g, C2, MU2, H2, buffer())
-                finish(planes, g, A0, WA - WC, C2, M2, H2)
+                    sums(planes, g, local, MU2, H2, buffer())
+                finish(planes, g, steps, local, A0, shift, M2, H2)
             return body
 
         def back_one_sums(planes):
-            g = [pack(score_adjoint(q, A1, 0, MU1, SG1)) for q in planes]
-            sums(planes, g, C, MU1, H1, buffer())
+            steps, local = start_of(planes, A1, 0, C)
+            g = [pack(score_adjoint(q, da, MU1, SG1)) for q, da in zip(planes, steps)]
+            sums(planes, g, local, MU1, H1, buffer())
             for d, q in enumerate(planes):
                 for b in range(nv + 1):
                     GS[q, pl.ds(8 * b, 8)] = g[d][b]
 
         def back_one_rest(planes):
+            steps, local = start_of(planes, A1, 0, C)
             g = [[GS[q, pl.ds(8 * b, 8)] for b in range(nv + 1)] for q in planes]
-            finish(planes, g, A1, 0, C, M1, H1)
+            finish(planes, g, steps, local, A1, 0, M1, H1)
 
         def back_one_sides(planes):
-            g = [pack(score_adjoint(q, A1, 0, MU1, SG1)) for q in planes]
-            finish(planes, g, A1, 0, C, M1, H1)
+            steps, local = start_of(planes, A1, 0, C)
+            g = [pack(score_adjoint(q, da, MU1, SG1)) for q, da in zip(planes, steps)]
+            finish(planes, g, steps, local, A1, 0, M1, H1)
 
         def join(p):
             A1[p] = RR[p] + UU[p - 1] + VV[p + 1]
 
         local_c.wait()
+        inner(1, forward_one_early)
         wait_for(halo_c, "y")
-        inner(1, forward_one)
+        inner(1, lambda planes: forward_one(planes, True))
         inner(2, advance)
         inner(3, forward_two)
         local_a.wait()
         wait_for(halo_a, "y")
+        for dz, dy, _ in PIECES_A:
+            if dz != 0:
+                halo_a[dz, dy, 0].start()
         inner(4, back_two(True))
         wait_for(halo_c, "z")
         outer(1, 6, forward_one)
@@ -469,14 +508,12 @@
     return kernel, yr, size1, size2
 
 
-def hand_over(field, sums, out, out_wi, out_bi, out_wo, out_bo, sem):
-    copy = pltpu.make_async_copy(field, out, sem)
-    copy.start()
+def hand_over(field, sums, out, out_wi, out_bi, out_wo, out_bo):
+    out[...] = field[...]
     out_wi[...] = sums[0:4, 0:UNITS]
     out_bi[...] = sums[4:5, 0:UNITS]
     out_wo[...] = sums[5:6, 0:UNITS]
     out_bo[...] = sums[6:7, 0:1]
-    copy.wait()
 
 
 def per_device(ng, ny, concentration, cotangent, w_in, b_in, w_out, b_out):
@@ -518,8 +555,8 @@
             pltpu.VMEM((max(size2, 1), 8, 128), F32),
             pltpu.VMEM((8, 128), F32),
             pltpu.VMEM((8, 128), F32),
-            pltpu.SemaphoreType.DMA((2, 8)),
-            pltpu.SemaphoreType.DMA((2, 8)),
+            pltpu.SemaphoreType.DMA((2, 12)),
+            pltpu.SemaphoreType.DMA((2, 12)),
             pltpu.SemaphoreType.DMA((3,)),
             pltpu.SemaphoreType.DMA((size1,)),
             pltpu.SemaphoreType.DMA((size1,)),
@@ -541,9 +578,8 @@
             jax.ShapeDtypeStruct((1, UNITS), F32),
             jax.ShapeDtypeStruct((1, 1), F32),
         ),
-        in_specs=[anywhere, vmem],
-        out_specs=(anywhere, vmem, vmem, vmem, vmem),
-        scratch_shapes=[pltpu.SemaphoreType.DMA],
+        in_specs=[vmem, vmem],
+        out_specs=(vmem, vmem, vmem, vmem, vmem),
     )(*outs)
     return (outs[0], outs[1].T, outs[2].reshape(UNITS), outs[3].reshape(UNITS), outs[4].reshape(()))
 

time: 58.6 us -> 47.8 us (0.82)
  Pallas kernels: 56.9 us -> 46.4 us
    pallas_call x1, Pallas kernels: 10.3 us -> 1.68 us  [per_device(): pl.pallas_call(hand_over, out_shape=(jax.ShapeDtypeStruct(concentration.s...]
    pallas_call x1, Pallas kernels: 46.6 us -> 44.7 us  [per_device(): pl.pallas_call(kernel, out_shape=(jax.ShapeDtypeStruct(concentration.shap...]
where the time goes in v2:
time: 47.8 us; the launch traced here: 47.7 us
  Pallas kernels  46.4 us (97%)
  between operations  1.29 us (3%)
    pallas_call x1, Pallas kernels, per_device(): pl.pallas_call(kernel, out_shape=(jax.ShapeDtypeStruct(concentration.shap...  44.7 us
    pallas_call x1, Pallas kernels, per_device(): pl.pallas_call(hand_over, out_shape=(jax.ShapeDtypeStruct(concentration.s...  1.68 us

profile of v2, /device:TPU:1, one launch (start us, length us, event | category | flops | bytes accessed | tf_op | source)
XLA Modules:
  0.0 47.7 jit_solution(15556077685344259524)
XLA Ops:
  1.3 44.7 %shard_map.101 = (f32[16,32,128]{2,1,0:T(8,128)}, f32[8,128]{1,0:T(8,128)}) custom-call(f32[16,32,128]{2,1,0:T(8,128)} %conc.1, f32[16,32,128]{2,1,0:T(8,128)} %cot.1, f32[4,32]{1,0:T(4,128)} %bitcast.9, f32[1,32]{1,0:T(1,128)} %bitcast.10, f32[1,32]{1,0:T(1,128)} %bitcast.11, f32[1,1]{1,0:T(1,128)} %bitcast.8.b_out), custom_call_target="tpu_custom_call" | custom-call | tf_op jit(solution)/shard_map/pallas_call | solution.py:529
  46.0 1.7 %shard_map.102 = (f32[16,32,128]{2,1,0:T(8,128)}, f32[4,32]{1,0:T(4,128)}, f32[1,32]{1,0:T(1,128)}, f32[1,32]{1,0:T(1,128)}, f32[1,1]{1,0:T(1,128)}) custom-call(f32[16,32,128]{2,1,0:T(8,128)} %get-tuple-element.12.field, f32[8,128]{1,0:T(8,128)} %get-tuple-element.13.sums), custom_call_target="tpu_custom_call" | custom-call | tf_op jit(solution)/shard_map/pallas_call | solution.py:572

commit v3 on v2

--- a/solution.py
+++ b/solution.py
@@ -148,10 +148,8 @@
 
         halo_c = halo(0, conc, C, PIECES_C, WC, 8, CORNER_C)
         halo_a = halo(1, cot, A0, PIECES_A, WA, 4, CORNER_A)
-        for copy in halo_c.values():
-            copy.start()
         for dy in (-1, 1):
-            halo_a[0, dy, 0].start()
+            halo_c[0, dy, 0].start()
 
         lane = iota((UNITS, 128), 1)
         eye = iota((UNITS, UNITS), 0) == iota((UNITS, UNITS), 1)
@@ -360,10 +358,14 @@
             TACC[...] = total.reshape(ROWS, 128)
             GACC[...] = g_total
 
-        def finish(planes, g, steps, local, adj, shift, m_ref, h_ref):
+        def finish(planes, g, steps, local, adj, shift, m_ref, h_ref, ub=None):
             A = [[None] * (nv + 1) for _ in planes]
-            for places in places_of(True, True):
-                back = dot(CT[...], hidden(planes, places, h_ref).astype(BF16))
+            for n, places in enumerate(places_of(True, True)):
+                if ub is not None and n < nv:
+                    u_high = ub[pl.ds(0, ROWS), pl.ds(256 * n, 256)]
+                else:
+                    u_high = hidden(planes, places, h_ref).astype(BF16)
+                back = dot(CT[...], u_high)
                 back = back[:32] + back[32:]
                 for i, (d, b) in enumerate(places):
                     A[d][b] = [back[8 * k:8 * k + 8, 128 * i:128 * i + 128] * g[d][b] for k in range(4)]
@@ -393,9 +395,10 @@
                 shift = WA - WC
                 steps, local = start_of(planes, A0, shift, C2)
                 g = [pack(score_adjoint(q, da, MU2, SG2)) for q, da in zip(planes, steps)]
+                ub = buffer() if with_sums else None
                 if with_sums:
-                    sums(planes, g, local, MU2, H2, buffer())
-                finish(planes, g, steps, local, A0, shift, M2, H2)
+                    sums(planes, g, local, MU2, H2, ub)
+                finish(planes, g, steps, local, A0, shift, M2, H2, ub)
             return body
 
         def back_one_sums(planes):
@@ -419,9 +422,14 @@
         def join(p):
             A1[p] = RR[p] + UU[p - 1] + VV[p + 1]
 
+        for dz, dy, part in PIECES_C:
+            if dz != 0:
+                halo_c[dz, dy, part].start()
         local_c.wait()
         inner(1, forward_one_early)
         wait_for(halo_c, "y")
+        for dy in (-1, 1):
+            halo_a[0, dy, 0].start()
         inner(1, lambda planes: forward_one(planes, True))
         inner(2, advance)
         inner(3, forward_two)
@@ -431,6 +439,9 @@
             if dz != 0:
                 halo_a[dz, dy, 0].start()
         inner(4, back_two(True))
+        for p in range(low + 5, high - 4):
+            join(p)
+        inner(6, back_one_sums)
         wait_for(halo_c, "z")
         outer(1, 6, forward_one)
         outer(2, 5, advance)
@@ -438,9 +449,9 @@
         wait_for(halo_a, "z")
         outer(4, 0, back_two(True))
         outer(0, 3, back_two(False))
-        for p in range(low - 2, high + 3):
+        for p in [*range(low - 2, low + 5), *range(high - 4, high + 3)]:
             join(p)
-        inner(0, back_one_sums)
+        outer(6, 0, back_one_sums)
 
         both = PACC[pl.ds(0, ROWS)] + PACC[pl.ds(ROWS, ROWS)]
         both = jnp.where(same & (col < 96), both, 0.0)
@@ -485,20 +496,18 @@
         sent1 = exchange(size1, place1, peer1, MSG, RED, rs_send, rs_recv)
 
         outer(0, 1, back_one_sides)
-        inner(0, back_one_rest)
+        inner(4, back_one_rest)
+        total = collected(size1, peer1, sent1, MSG, RED, rs_send, rs_recv)
+        MSG2[...] = total
+        sent2 = exchange(size2, place2, peer2, MSG2, RED2, rs2_send, rs2_recv)
+        outer(4, 0, back_one_rest)
         for p in range(low, high + 1):
             rows = pl.ds(R, yl)
             OUTV[p - WC] = RR[p, rows] + UU[p - 1, rows] + VV[p + 1, rows]
         write = pltpu.make_async_copy(OUTV, out, local_sem.at[2])
         write.start()
 
-        total = collected(size1, peer1, sent1, MSG, RED, rs_send, rs_recv)
-        MSG2[...] = total
-        if size2 > 1:
-            sent2 = exchange(size2, place2, peer2, MSG2, RED2, rs2_send, rs2_recv)
-            total = collected(size2, peer2, sent2, MSG2, RED2, rs2_send, rs2_recv)
-        else:
-            sent2 = []
+        total = collected(size2, peer2, sent2, MSG2, RED2, rs2_send, rs2_recv)
         out_sums[...] = total * factor
 
         for copy in [*halo_c.values(), *halo_a.values(), *sent1, *sent2]:

time: 47.8 us -> 46.9 us (0.981)
  Pallas kernels: 46.4 us -> 45.5 us
    pallas_call x1, Pallas kernels: 44.7 us -> 43.8 us  [per_device(): pl.pallas_call(kernel, out_shape=(jax.ShapeDtypeStruct(concentration.shap...]
where the time goes in v3:
time: 46.9 us; the launch traced here: 46.7 us
  Pallas kernels  45.5 us (97%)
  between operations  1.29 us (3%)
    pallas_call x1, Pallas kernels, per_device(): pl.pallas_call(kernel, out_shape=(jax.ShapeDtypeStruct(concentration.shap...  43.8 us
    pallas_call x1, Pallas kernels, per_device(): pl.pallas_call(hand_over, out_shape=(jax.ShapeDtypeStruct(concentration.s...  1.68 us

profile of v3, /device:TPU:1, one launch (start us, length us, event | category | flops | bytes accessed | tf_op | source)
XLA Modules:
  0.0 46.7 jit_solution(12002968915715646850)
XLA Ops:
  1.3 43.8 %shard_map.101 = (f32[16,32,128]{2,1,0:T(8,128)}, f32[8,128]{1,0:T(8,128)}) custom-call(f32[16,32,128]{2,1,0:T(8,128)} %conc.1, f32[16,32,128]{2,1,0:T(8,128)} %cot.1, f32[4,32]{1,0:T(4,128)} %bitcast.9, f32[1,32]{1,0:T(1,128)} %bitcast.10, f32[1,32]{1,0:T(1,128)} %bitcast.11, f32[1,1]{1,0:T(1,128)} %bitcast.8.b_out), custom_call_target="tpu_custom_call" | custom-call | tf_op jit(solution)/shard_map/pallas_call | solution.py:538
  45.1 1.7 %shard_map.102 = (f32[16,32,128]{2,1,0:T(8,128)}, f32[4,32]{1,0:T(4,128)}, f32[1,32]{1,0:T(1,128)}, f32[1,32]{1,0:T(1,128)}, f32[1,1]{1,0:T(1,128)}) custom-call(f32[16,32,128]{2,1,0:T(8,128)} %get-tuple-element.12.field, f32[8,128]{1,0:T(8,128)} %get-tuple-element.13.sums), custom_call_target="tpu_custom_call" | custom-call | tf_op jit(solution)/shard_map/pallas_call | solution.py:581

commit v4 on v3

--- a/solution.py
+++ b/solution.py
@@ -468,11 +468,17 @@
         grads = jnp.where(lane == 5, t_col, grads)
         grads = jnp.where((lane == 6) & first_row, g_sum, grads)
         square = jnp.concatenate([grads, jnp.zeros((128 - UNITS, 128), F32)], axis=0)
-        MSG[...] = square.T[0:8]
-
-        def exchange(size, place, peer, src, slots, s_sem, r_sem):
+        by_kind = square.T[0:8]
+        kind = iota((8, 128), 0)
+        lined = jnp.zeros((8, 128), F32)
+        for k in range(4):
+            lined = jnp.where((kind & 3) == k, pltpu.roll(by_kind, 32 * k, 1) if k else by_kind, lined)
+        MSG[...] = jnp.concatenate([
+            jnp.sum(lined[4 * n:4 * n + 4], axis=0, keepdims=True) for n in range(2)], axis=0)
+
+        def exchange(size, ring, place, peer, src, slots, s_sem, r_sem):
             copies = []
-            for k in range(1, size):
+            for k in sorted(range(1, size), key=lambda k: abs(k % ring - ring // 2)):
                 q, device = peer(k)
                 copy = pltpu.make_async_remote_copy(
                     src_ref=src, dst_ref=slots.at[place], send_sem=s_sem.at[k],
@@ -493,13 +499,13 @@
                 total = total + slots[k]
             return total
 
-        sent1 = exchange(size1, place1, peer1, MSG, RED, rs_send, rs_recv)
+        sent1 = exchange(size1, n_z, place1, peer1, MSG, RED, rs_send, rs_recv)
 
         outer(0, 1, back_one_sides)
         inner(4, back_one_rest)
         total = collected(size1, peer1, sent1, MSG, RED, rs_send, rs_recv)
         MSG2[...] = total
-        sent2 = exchange(size2, place2, peer2, MSG2, RED2, rs2_send, rs2_recv)
+        sent2 = exchange(size2, 4, place2, peer2, MSG2, RED2, rs2_send, rs2_recv)
         outer(4, 0, back_one_rest)
         for p in range(low, high + 1):
             rows = pl.ds(R, yl)
@@ -508,7 +514,12 @@
         write.start()
 
         total = collected(size2, peer2, sent2, MSG2, RED2, rs2_send, rs2_recv)
-        out_sums[...] = total * factor
+        total = total * factor
+        spread_rows = jnp.where(kind < 4, total[0:1], total[1:2])
+        sums_out = jnp.zeros((8, 128), F32)
+        for k in range(4):
+            sums_out = jnp.where((kind & 3) == k, pltpu.roll(spread_rows, 128 - 32 * k, 1) if k else spread_rows, sums_out)
+        out_sums[...] = sums_out
 
         for copy in [*halo_c.values(), *halo_a.values(), *sent1, *sent2]:
             copy.wait_send()
@@ -560,10 +571,10 @@
             pltpu.VMEM((ROWS, 128), F32),
             pltpu.VMEM((8, 128), F32),
             pltpu.VMEM((zl, yl, nx), F32),
-            pltpu.VMEM((size1, 8, 128), F32),
-            pltpu.VMEM((max(size2, 1), 8, 128), F32),
-            pltpu.VMEM((8, 128), F32),
-            pltpu.VMEM((8, 128), F32),
+            pltpu.VMEM((size1, 2, 128), F32),
+            pltpu.VMEM((max(size2, 1), 2, 128), F32),
+            pltpu.VMEM((2, 128), F32),
+            pltpu.VMEM((2, 128), F32),
             pltpu.SemaphoreType.DMA((2, 12)),
             pltpu.SemaphoreType.DMA((2, 12)),
             pltpu.SemaphoreType.DMA((3,)),

time: 46.9 us -> 46.3 us (0.987)
  Pallas kernels: 45.5 us -> 44.9 us
    pallas_call x1, Pallas kernels: 43.8 us -> 43.2 us  [per_device(): pl.pallas_call(kernel, out_shape=(jax.ShapeDtypeStruct(concentration.shap...]
where the time goes in v4:
time: 46.3 us; the launch traced here: 46.2 us
  Pallas kernels  44.9 us (97%)
  between operations  1.29 us (3%)
    pallas_call x1, Pallas kernels, per_device(): pl.pallas_call(kernel, out_shape=(jax.ShapeDtypeStruct(concentration.shap...  43.2 us
    pallas_call x1, Pallas kernels, per_device(): pl.pallas_call(hand_over, out_shape=(jax.ShapeDtypeStruct(concentration.s...  1.68 us

profile of v4, /device:TPU:1, one launch (start us, length us, event | category | flops | bytes accessed | tf_op | source)
XLA Modules:
  0.0 46.2 jit_solution(17367250948505866218)
XLA Ops:
  1.3 43.2 %shard_map.101 = (f32[16,32,128]{2,1,0:T(8,128)}, f32[8,128]{1,0:T(8,128)}) custom-call(f32[16,32,128]{2,1,0:T(8,128)} %conc.1, f32[16,32,128]{2,1,0:T(8,128)} %cot.1, f32[4,32]{1,0:T(4,128)} %bitcast.9, f32[1,32]{1,0:T(1,128)} %bitcast.10, f32[1,32]{1,0:T(1,128)} %bitcast.11, f32[1,1]{1,0:T(1,128)} %bitcast.8.b_out), custom_call_target="tpu_custom_call" | custom-call | tf_op jit(solution)/shard_map/pallas_call | solution.py:549
  44.5 1.7 %shard_map.102 = (f32[16,32,128]{2,1,0:T(8,128)}, f32[4,32]{1,0:T(4,128)}, f32[1,32]{1,0:T(1,128)}, f32[1,32]{1,0:T(1,128)}, f32[1,1]{1,0:T(1,128)}) custom-call(f32[16,32,128]{2,1,0:T(8,128)} %get-tuple-element.12.field, f32[8,128]{1,0:T(8,128)} %get-tuple-element.13.sums), custom_call_target="tpu_custom_call" | custom-call | tf_op jit(solution)/shard_map/pallas_call | solution.py:592

commit v5 on v4

--- a/solution.py
+++ b/solution.py
@@ -98,17 +98,6 @@
             cot, A0.at[pl.ds(WA, zl), pl.ds(R, yl)], local_sem.at[1])
         local_c.start()
         local_a.start()
-
-        for margin in (0, R + yl):
-            for first, length in ((0, WC - 2), (WC + zl + 2, WC - 2)):
-                rows = pl.ds(margin + (0 if margin == 0 else 4), 4)
-                C[pl.ds(first, length), rows] = jnp.zeros((length, 4, 128), F32)
-            for p in (0, 2 * WC + zl - 1):
-                C[p, pl.ds(margin, R)] = jnp.zeros((R, 128), F32)
-            rows = pl.ds(margin + (0 if margin == 0 else 4), 4)
-            A0[:, rows] = jnp.zeros((zl + 2 * WA, 4, 128), F32)
-            for p in (0, 2 * WA + zl - 1):
-                A0[p, pl.ds(margin, R)] = jnp.zeros((R, 128), F32)
 
         barrier = pltpu.get_barrier_semaphore()
         count = 0
@@ -150,6 +139,17 @@
         halo_a = halo(1, cot, A0, PIECES_A, WA, 4, CORNER_A)
         for dy in (-1, 1):
             halo_c[0, dy, 0].start()
+
+        for margin in (0, R + yl):
+            for first, length in ((0, WC - 2), (WC + zl + 2, WC - 2)):
+                rows = pl.ds(margin + (0 if margin == 0 else 4), 4)
+                C[pl.ds(first, length), rows] = jnp.zeros((length, 4, 128), F32)
+            for p in (0, 2 * WC + zl - 1):
+                C[p, pl.ds(margin, R)] = jnp.zeros((R, 128), F32)
+            rows = pl.ds(margin + (0 if margin == 0 else 4), 4)
+            A0[:, rows] = jnp.zeros((zl + 2 * WA, 4, 128), F32)
+            for p in (0, 2 * WA + zl - 1):
+                A0[p, pl.ds(margin, R)] = jnp.zeros((R, 128), F32)
 
         lane = iota((UNITS, 128), 1)
         eye = iota((UNITS, UNITS), 0) == iota((UNITS, UNITS), 1)
@@ -243,7 +243,7 @@
                 for i in range(2, nv, 2):
                     forward_blocks(q, feats, (i, i + 1), R)
 
-        def forward_one(planes, early=False):
+        def forward_one(planes, early=False, sides=True):
             for q in planes:
                 c, lap, sq, _ = fields_of(C, q)
                 mu = c * c * c - c - KAPPA * lap
@@ -253,7 +253,11 @@
                     for i in range(2, nv, 2):
                         forward_blocks(q, feats, (i, i + 1), 0)
                 forward_blocks(q, feats, (1, nv), 0)
-                forward_blocks(q, feats, (nv + 1, 0), 0)
+                if sides:
+                    forward_blocks(q, feats, (nv + 1, 0), 0)
+                else:
+                    for i in (0, nv + 1):
+                        M1[q, pl.ds(8 * i, 8)] = jnp.zeros((8, 128), F32)
 
         def wait_for(copies, sides):
             for dz, dy, part in copies:
@@ -443,7 +447,8 @@
             join(p)
         inner(6, back_one_sums)
         wait_for(halo_c, "z")
-        outer(1, 6, forward_one)
+        outer(1, 5, forward_one)
+        forward_one((low - 6, high + 6), sides=False)
         outer(2, 5, advance)
         outer(3, 4, forward_two)
         wait_for(halo_a, "z")

time: 46.3 us -> 46.1 us (level)
  no operation moved by 1% of the time
where the time goes in v5:
time: 46.1 us; the launch traced here: 46 us
  Pallas kernels  44.7 us (97%)
  between operations  1.29 us (3%)
    pallas_call x1, Pallas kernels, per_device(): pl.pallas_call(kernel, out_shape=(jax.ShapeDtypeStruct(concentration.shap...  43 us
    pallas_call x1, Pallas kernels, per_device(): pl.pallas_call(hand_over, out_shape=(jax.ShapeDtypeStruct(concentration.s...  1.68 us

profile of v5, /device:TPU:1, one launch (start us, length us, event | category | flops | bytes accessed | tf_op | source)
XLA Modules:
  0.0 46.0 jit_solution(1442461385155812342)
XLA Ops:
  1.3 43.0 %shard_map.101 = (f32[16,32,128]{2,1,0:T(8,128)}, f32[8,128]{1,0:T(8,128)}) custom-call(f32[16,32,128]{2,1,0:T(8,128)} %conc.1, f32[16,32,128]{2,1,0:T(8,128)} %cot.1, f32[4,32]{1,0:T(4,128)} %bitcast.9, f32[1,32]{1,0:T(1,128)} %bitcast.10, f32[1,32]{1,0:T(1,128)} %bitcast.11, f32[1,1]{1,0:T(1,128)} %bitcast.8.b_out), custom_call_target="tpu_custom_call" | custom-call | tf_op jit(solution)/shard_map/pallas_call | solution.py:554
  44.3 1.7 %shard_map.102 = (f32[16,32,128]{2,1,0:T(8,128)}, f32[4,32]{1,0:T(4,128)}, f32[1,32]{1,0:T(1,128)}, f32[1,32]{1,0:T(1,128)}, f32[1,1]{1,0:T(1,128)}) custom-call(f32[16,32,128]{2,1,0:T(8,128)} %get-tuple-element.12.field, f32[8,128]{1,0:T(8,128)} %get-tuple-element.13.sums), custom_call_target="tpu_custom_call" | custom-call | tf_op jit(solution)/shard_map/pallas_call | solution.py:597
